TPU v7x, 32 devices: a whole 2x2x4 slice. The times are simulated.
32 devices in a mesh: groups: 2 (over y), layer: 4 (over z), dp: 2 (over x), chan: 2 (over core).
Axes of the slice: x: 2, y: 2, z: 4, core: 2. Of those that a mesh axis runs over, the one named last changes fastest.
Arguments:
- activations: bfloat16 [4, 4, 32, 16, 16, 128], P('layer', None, ('groups', 'dp', 'chan')), parts along dimension 2, may hold values from -0.94921875 to 0.94921875
- weights: bfloat16 [4, 4, 9, 128, 128], P('layer'), may hold values from -0.1875 to 0.1875
- guesses: bfloat16 [4, 32, 16, 16, 128], P('layer', ('groups', 'dp', 'chan')), parts along dimension 1, may hold values from -6 to 6
- terminal: bfloat16 [32, 16, 16, 128], P(('groups', 'dp', 'chan')), parts along dimension 0, may hold values from -6 to 6
- coarse_rates: float32 [4, 128], P('layer'), may hold values from 0.0074 to 1, as said below
- block_layers: int32 [4], P('layer'), may hold values from 1 to 4, 12 in all
Outputs:
- corrected: bfloat16 [4, 32, 16, 16, 128], P('layer', ('groups', 'dp', 'chan')), parts along dimension 1
- kernel_grads: bfloat16 [8, 4, 9, 128, 128], P(('groups', 'layer')), parts along dimension 0
There are 2 independent parts, one for each index of `groups`. A program takes and returns all parts, laid end to end along the dimension named above; an argument that names none is the same for every part. Nothing has to cross between parts.
Inputs may be any that keep to these rules, and one draw needn't show every extreme that they name: `block_layers`: every block holds at least one layer and some block holds exactly 4; the counts sum to 12. `coarse_rates`: strictly positive.
All inputs are finite; a program needn't handle non-finite values.
Results may differ from a plain program's by a relative error of at most 0.0055.
Values may be sent and summed in bfloat16 or wider, within the bound.
A program may use at most 64 MiB of HBM per device.

v0:
```python
import jax
import jax.numpy as jnp
from jax import lax
from jax.sharding import PartitionSpec as P

MMAX = 4
step_size = 0.25
OFFSETS = [(row_off, col_off) for row_off in (-1, 0, 1) for col_off in (-1, 0, 1)]


def shifted(value, axis, steps):
    count = lax.axis_size(axis)
    first, last = (max(0, -steps), min(count, count - steps))
    return lax.ppermute(value, axis, [(source, source + steps) for source in range(first, last)])


def entering(part, axis, combine, identity):
    count = lax.axis_size(axis)
    place = lax.axis_index(axis)
    ahead = count - 1 - place
    gathered = jax.tree.map(lambda a: lax.all_gather(a, axis), part)
    state = jax.tree.map(lambda a, e: jnp.zeros_like(a) + jnp.asarray(e, a.dtype), part, identity)

    def one(turn, state):
        source = count - 1 - turn
        return combine(
            state, jax.tree.map(lambda a: lax.dynamic_index_in_dim(a, source, 0, False), gathered)
        )

    return lax.fori_loop(0, ahead, one, state)


def adjoint_step(adjoint, activation, kernel):
    map_side = adjoint.shape[1]
    rounded = adjoint.astype(jnp.bfloat16)
    padded = jnp.pad(rounded, ((0, 0), (1, 1), (1, 1), (0, 0)))
    summed = jnp.zeros(adjoint.shape, jnp.float32)
    for index, (row_off, col_off) in enumerate(OFFSETS):
        sliced = padded[
            :, 1 - row_off : 1 - row_off + map_side, 1 - col_off : 1 - col_off + map_side, :
        ]
        summed = summed + jnp.dot(sliced, kernel[index].T, preferred_element_type=jnp.float32)
    act_float = activation.astype(jnp.float32)
    return (adjoint + step_size * (1.0 - act_float * act_float) * summed, rounded)


def kernel_grad(activation, rounded):
    map_side = rounded.shape[1]
    padded = jnp.pad(activation, ((0, 0), (1, 1), (1, 1), (0, 0)))
    pieces = []
    for row_off, col_off in OFFSETS:
        sliced = padded[
            :, 1 + row_off : 1 + row_off + map_side, 1 + col_off : 1 + col_off + map_side, :
        ]
        pieces.append(
            lax.dot_general(
                sliced,
                rounded,
                (((0, 1, 2), (0, 1, 2)), ((), ())),
                preferred_element_type=jnp.float32,
            )
        )
    return step_size * jnp.stack(pieces)


def per_device(activations, weights, guesses, terminal, coarse_rates, block_layers):
    layer_count = block_layers[0]
    acts_block = activations[0]
    kernels_block = weights[0]
    at_end = lax.axis_index("layer") == lax.axis_size("layer") - 1
    end_state = terminal.astype(jnp.float32)
    own_guess = guesses[0].astype(jnp.float32)
    received = shifted(guesses, "layer", -1)[0]
    adjoint = jnp.where(at_end, end_state, received.astype(jnp.float32))
    for slot in reversed(range(MMAX)):
        stepped, _ = adjoint_step(adjoint, acts_block[slot], kernels_block[slot])
        adjoint = jnp.where(slot < layer_count, stepped, adjoint)
    residual = adjoint - own_guess
    rates = coarse_rates[0]

    def compose(earlier, later):
        return (later[0] * earlier[0], later[1] + later[0] * earlier[1])

    identity = (jnp.ones_like(rates), jnp.zeros_like(residual))
    _, following = entering((rates, residual), "layer", compose, identity)
    correction = residual + rates * following
    corrected = (own_guess + correction).astype(jnp.bfloat16)
    received = shifted(corrected[None], "layer", -1)[0]
    adjoint = jnp.where(at_end, end_state, received.astype(jnp.float32))
    slot_list = [None] * MMAX
    for slot in reversed(range(MMAX)):
        stepped, rounded = adjoint_step(adjoint, acts_block[slot], kernels_block[slot])
        active = slot < layer_count
        slot_grad = kernel_grad(acts_block[slot], rounded)
        slot_grad = jnp.where(active, slot_grad, jnp.zeros_like(slot_grad))
        slot_list[slot] = slot_grad
        adjoint = jnp.where(active, stepped, adjoint)
    stacked = jnp.stack(slot_list)
    result = lax.psum(stacked, ("dp", "chan")).astype(jnp.bfloat16)
    return (corrected[None], result[None])


def solution(mesh):
    in_specs = (
        P("layer", None, ("groups", "dp", "chan"), None, None, None),
        P("layer", None, None, None, None),
        P("layer", ("groups", "dp", "chan"), None, None, None),
        P(("groups", "dp", "chan"), None, None, None),
        P("layer", None),
        P("layer"),
    )
    out_specs = (
        P("layer", ("groups", "dp", "chan"), None, None, None),
        P(("groups", "layer"), None, None, None, None),
    )
    return jax.shard_map(
        per_device, mesh=mesh, in_specs=in_specs, out_specs=out_specs, check_vma=False
    )
```

profile of v0, /device:TPU:0, one launch (start us, length us, event | category | flops | bytes accessed | tf_op | source)
XLA Modules:
  0.0 162.6 jit_solution(5716062791998601039)
XLA Ops:
  7.2 1.4 collective-permute-start
  9.3 9.5 %collective-permute-done = bf16[1,4,16,16,128]{4,3,2,1,0:T(8,128)(2,1)S(1)} collective-permute-done((bf16[1,4,16,16,128]{4,3,2,1,0:T(8,128)(2,1)}, bf16[1,4,16,16,128]{4,3,2,1,0:T(8,128)(2,1)S(1)}, u32[]{:S(2)}, u32[]{:S(2)}) %collective-permute-start) | collective-permute-done | bytes 262176 | tf_op jit(solution)/shard_map/ppermute | solution.py:14
  18.8 1.0 fusion.60
  19.8 1.0 fusion.63
  22.5 0.7 copy-done
  23.3 0.3 fusion.284
  25.5 0.3 fusion.285
  27.7 0.3 fusion.286
  29.9 0.5 copy-done.4
  30.4 1.1 fusion.12
  31.5 9.3 %all-gather.1 = f32[4,1,128]{2,1,0:T(1,128)S(1)} all-gather(f32[1,1,128]{2,1,0:T(1,128)S(1)} %bitcast.708), channel_id=1, replica_groups=mesh['groups'=2,'layer'=4,'dp'=2,'chan'=2] {'layer'}, dimensions={0}, use_global_device_ids=true | all-gather | bytes 2560 | tf_op jit(solution)/shard_map/all_gather | solution.py:21
  40.9 37.1 %all-gather.4.cloned.1.call-done = f32[16,16,16,128]{3,2,1,0:T(8,128)} async-done(((f32[4,16,16,128]{3,2,1,0:T(8,128)}), f32[16,16,16,128]{3,2,1,0:T(8,128)}) %all-gather.4.cloned.1.call-update) | async-done | bytes 2097168 | tf_op jit(solution)/shard_map/all_gather | solution.py:21
  78.0 3.9 %while.14 = (s32[]{:T(128)}, f32[4,16,16,128]{3,2,1,0:T(8,128)S(1)}, s32[]{:T(128)}, f32[4,4,16,16,128]{4,3,2,1,0:T(8,128)}, f32[4,128]{1,0:T(4,128)S(1)}, /*index=5*/s32[]{:T(128)}, s32[]{:T(128)}, s32[]{:T(128)}, s32[]{:T(128)}) while((s32[]{:T(128)}, f32[4,16,16,128]{3,2,1,0:T(8,128)S(1)}, s32[]{:T(128)}, f32[4,4,16,16,128]{4,3,2,1,0:T(8,128)}, ...), condition=%wide.region_1.2_spmd, body=%wide.region_0.1_spmd.sunk | while | flops 262150 | bytes 1574555 | solution.py:30
  78.1 1.3 bitcast_add_fusion.2
  79.4 1.2 bitcast_add_fusion.2
  80.7 1.2 bitcast_add_fusion.2
  82.0 1.0 fusion.62
  83.0 1.5 collective-permute-start.1
  84.7 8.3 %collective-permute-done.1 = bf16[1,4,16,16,128]{4,3,2,1,0:T(8,128)(2,1)S(1)} collective-permute-done((bf16[1,4,16,16,128]{4,3,2,1,0:T(8,128)(2,1)S(1)}, bf16[1,4,16,16,128]{4,3,2,1,0:T(8,128)(2,1)S(1)}, u32[]{:S(2)}, u32[]{:S(2)}) %collective-permute-start.1) | collective-permute-done | bytes 262176 | tf_op jit(solution)/shard_map/ppermute | solution.py:14
  94.9 0.3 fusion.287
  97.2 0.3 fusion.288
  99.4 0.3 fusion.22
  100.8 0.3 fusion.54
  101.3 0.3 fusion.52
  101.6 0.3 fusion.51
  101.9 0.3 fusion.50
  103.3 0.3 fusion.36
  103.9 0.3 fusion.34
  105.8 0.3 fusion.27
  106.4 0.3 fusion.25
  108.4 0.3 fusion.45
  110.3 45.5 %all-reduce.12 = bf16[4,9,128,128]{3,2,1,0:T(8,128)(2,1)} all-reduce(f32[4,9,128,128]{3,2,1,0:T(8,128)S(1)} %pad_maximum_fusion), channel_id=1, replica_groups=mesh['groups'=2,'layer'=4,'dp'=2,'chan'=2] {'dp','chan'}, use_global_device_ids=true, to_apply=%region_2.3 | all-reduce | flops 589824 | bytes 3538944 | tf_op jit(solution)/shard_map/psum | solution.py:99
  (105 shorter events, 21.0 us)
Async XLA Ops:
  7.2 13.7 %copy-start.3 = (bf16[1,4,9,128,128]{4,3,2,1,0:T(8,128)(2,1)S(1)}, bf16[1,4,9,128,128]{4,3,2,1,0:T(8,128)(2,1)}, u32[]{:S(2)}) copy-start(bf16[1,4,9,128,128]{4,3,2,1,0:T(8,128)(2,1)} %param.9) | copy-start | bytes 3538948
  7.2 70.8 %all-gather.4.cloned.1.call-start = ((), (), s32[]{:S(2)}) async-start(), calls=%async_computation | async-start | bytes 2621440 | tf_op jit(solution)/shard_map/all_gather | solution.py:21
  7.2 11.6 %collective-permute-start = (bf16[1,4,16,16,128]{4,3,2,1,0:T(8,128)(2,1)}, bf16[1,4,16,16,128]{4,3,2,1,0:T(8,128)(2,1)S(1)}, u32[]{:S(2)}, u32[]{:S(2)}) collective-permute-start(bf16[1,4,16,16,128]{4,3,2,1,0:T(8,128)(2,1)} %param.10), channel_id=1, source_target_pairs={{4,0},{8,4},{12,8},{5,1},{9,5},{13,9},{6,2},{10,6},{14,10},{7,3},{... | collective-permute-start | bytes 786440 | tf_op jit(solution)/shard_map/ppermute | solution.py:14
  22.0 1.2 copy-start
  22.0 1.3 copy-start.2
  29.4 1.0 copy-start.4
  30.4 1.1 copy-start.6
  78.0 3.9 %copy-start.1 = (f32[4,16,16,128]{3,2,1,0:T(8,128)S(1)}, f32[4,16,16,128]{3,2,1,0:T(8,128)}, u32[]{:S(2)}) copy-start(f32[4,16,16,128]{3,2,1,0:T(8,128)} %fusion.12) | copy-start | bytes 1572868
  83.0 10.0 %copy-start.5 = (bf16[1,4,16,16,128]{4,3,2,1,0:T(8,128)(2,1)}, bf16[1,4,16,16,128]{4,3,2,1,0:T(8,128)(2,1)S(1)}, u32[]{:S(2)}) copy-start(bf16[1,4,16,16,128]{4,3,2,1,0:T(8,128)(2,1)S(1)} %fusion.62) | copy-start | bytes 786436
  83.0 9.9 %collective-permute-start.1 = (bf16[1,4,16,16,128]{4,3,2,1,0:T(8,128)(2,1)S(1)}, bf16[1,4,16,16,128]{4,3,2,1,0:T(8,128)(2,1)S(1)}, u32[]{:S(2)}, u32[]{:S(2)}) collective-permute-start(bf16[1,4,16,16,128]{4,3,2,1,0:T(8,128)(2,1)S(1)} %fusion.62), channel_id=1, source_target_pairs={{4,0},{8,4},{12,8},{5,1},{9,5},{13,9},{6,2},{10,6},{14,10},{7,3},{... | collective-permute-start | bytes 786440 | tf_op jit(solution)/shard_map/ppermute | solution.py:14
Sparse Core Ops, SparseCore 0:
  31.6 46.3 all-gather.3
where the time goes:
time: 163 us
  waiting for transfers between devices  54.9 us (34%)
  blocking collectives  54.8 us (34%)
  matrix products  26.5 us (16%)
  between operations  15.5 us (10%)
  other arithmetic  6.39 us (4%)
  starting transfers between devices  2.93 us (2%)
    psum x1, blocking collectives, per_device(): result = lax.psum(stacked, ('dp', 'chan')).astype(jnp.bfloat16)  45.5 us
    all_gather x1, waiting for transfers between devices, entering(): gathered = jax.tree.map(lambda a: lax.all_gather(a, axis), part)  37.1 us
    ppermute x2, waiting for transfers between devices, shifted(): lax.ppermute(value, axis, [(source, source + steps) for source in range(f...  17.7 us
    dot_general x63, matrix products, adjoint_step(): jnp.dot(sliced, kernel[index].T, preferred_element_type=jnp.float32)  16.6 us
    dot_general x36, matrix products, kernel_grad(): lax.dot_general(sliced, rounded, (((0, 1, 2), (0, 1, 2)), ((), ())), pref...  9.87 us
    all_gather x1, blocking collectives, entering(): gathered = jax.tree.map(lambda a: lax.all_gather(a, axis), part)  9.34 us
    add x3, other arithmetic, compose(): return (later[0] * earlier[0], later[1] + later[0] * earlier[1])  3.78 us
  transfers between devices with their start and end apart: 3, of which 3 were waited for; matrix products, arithmetic and copies ran while one was open for 0% of the time, Pallas kernels for 0%

commit v1 on v0

--- a/solution.py
+++ b/solution.py
@@ -96,7 +96,7 @@
         slot_list[slot] = slot_grad
         adjoint = jnp.where(active, stepped, adjoint)
     stacked = jnp.stack(slot_list)
-    result = lax.psum(stacked, ("dp", "chan")).astype(jnp.bfloat16)
+    result = jnp.sum(lax.all_gather(stacked, ("dp", "chan")), axis=0).astype(jnp.bfloat16)
     return (corrected[None], result[None])
 
 

time: 163 us -> 188 us (1.15)
  waiting for transfers between devices: 54.9 us -> 117 us
  blocking collectives: 54.8 us -> 9.34 us
  other arithmetic: 6.39 us -> 13.8 us
    all_gather x0 -> x1, waiting for transfers between devices: none -> 62.5 us  [per_device(): lax.all_gather(stacked, ('dp', 'chan'))]
    psum x1 -> x0, blocking collectives: 45.5 us -> none  [per_device(): result = lax.psum(stacked, ('dp', 'chan')).astype(jnp.bfloat16)]
    reduce_sum x0 -> x1, other arithmetic: none -> 6.03 us  [per_device(): jnp.sum(lax.all_gather(stacked, ('dp', 'chan')), axis=0)]
  transfers between devices with their start and end apart: 3 -> 4, of which waited for: 3 -> 4; matrix products, arithmetic and copies ran while one was open for 0% -> 0% of each run, Pallas kernels for 0% -> 0%
where the time goes in v1:
time: 188 us; the launch traced here: 187 us
  waiting for transfers between devices  117 us (62%)
  matrix products  26.4 us (14%)
  between operations  15.5 us (8%)
  other arithmetic  13.8 us (7%)
  blocking collectives  9.34 us (5%)
  starting transfers between devices  2.98 us (2%)
    all_gather x1, waiting for transfers between devices, per_device(): lax.all_gather(stacked, ('dp', 'chan'))  62.5 us
    all_gather x1, waiting for transfers between devices, entering(): gathered = jax.tree.map(lambda a: lax.all_gather(a, axis), part)  37.1 us
    ppermute x2, waiting for transfers between devices, shifted(): lax.ppermute(value, axis, [(source, source + steps) for source in range(f...  17.7 us
    dot_general x63, matrix products, adjoint_step(): jnp.dot(sliced, kernel[index].T, preferred_element_type=jnp.float32)  16.6 us
    dot_general x36, matrix products, kernel_grad(): lax.dot_general(sliced, rounded, (((0, 1, 2), (0, 1, 2)), ((), ())), pref...  9.81 us
    all_gather x1, blocking collectives, entering(): gathered = jax.tree.map(lambda a: lax.all_gather(a, axis), part)  9.34 us
    reduce_sum x1, other arithmetic, per_device(): jnp.sum(lax.all_gather(stacked, ('dp', 'chan')), axis=0)  6.03 us
    add x3, other arithmetic, compose(): return (later[0] * earlier[0], later[1] + later[0] * earlier[1])  3.78 us
  transfers between devices with their start and end apart: 4, of which 4 were waited for; matrix products, arithmetic and copies ran while one was open for 0% of the time, Pallas kernels for 0%

profile of v1, /device:TPU:0, one launch (start us, length us, event | category | flops | bytes accessed | tf_op | source)
XLA Modules:
  0.0 187.0 jit_solution(14316713710736795717)
XLA Ops:
  7.2 1.4 collective-permute-start
  9.3 9.5 %collective-permute-done = bf16[1,4,16,16,128]{4,3,2,1,0:T(8,128)(2,1)S(1)} collective-permute-done((bf16[1,4,16,16,128]{4,3,2,1,0:T(8,128)(2,1)}, bf16[1,4,16,16,128]{4,3,2,1,0:T(8,128)(2,1)S(1)}, u32[]{:S(2)}, u32[]{:S(2)}) %collective-permute-start) | collective-permute-done | bytes 262176 | tf_op jit(solution)/shard_map/ppermute | solution.py:14
  18.8 1.0 fusion.60
  19.8 1.0 fusion.63
  22.5 0.7 copy-done
  23.3 0.3 fusion.284
  25.5 0.3 fusion.285
  27.7 0.3 fusion.286
  29.9 0.5 copy-done.4
  30.4 1.1 fusion.12
  31.6 9.3 %all-gather.2 = f32[4,1,128]{2,1,0:T(1,128)S(1)} all-gather(f32[1,1,128]{2,1,0:T(1,128)S(1)} %bitcast.710), channel_id=1, replica_groups=mesh['groups'=2,'layer'=4,'dp'=2,'chan'=2] {'layer'}, dimensions={0}, use_global_device_ids=true | all-gather | bytes 2560 | tf_op jit(solution)/shard_map/all_gather | solution.py:21
  40.9 37.1 %all-gather.6.cloned.1.call-done = f32[16,16,16,128]{3,2,1,0:T(8,128)} async-done(((f32[4,16,16,128]{3,2,1,0:T(8,128)}), f32[16,16,16,128]{3,2,1,0:T(8,128)}) %all-gather.6.cloned.1.call-update) | async-done | bytes 2097168 | tf_op jit(solution)/shard_map/all_gather | solution.py:21
  78.0 3.9 %while.14 = (s32[]{:T(128)}, f32[4,16,16,128]{3,2,1,0:T(8,128)S(1)}, s32[]{:T(128)}, f32[4,4,16,16,128]{4,3,2,1,0:T(8,128)}, f32[4,128]{1,0:T(4,128)S(1)}, /*index=5*/s32[]{:T(128)}, s32[]{:T(128)}, s32[]{:T(128)}, s32[]{:T(128)}) while((s32[]{:T(128)}, f32[4,16,16,128]{3,2,1,0:T(8,128)S(1)}, s32[]{:T(128)}, f32[4,4,16,16,128]{4,3,2,1,0:T(8,128)}, ...), condition=%wide.region_1.2_spmd, body=%wide.region_0.1_spmd.sunk | while | flops 262150 | bytes 1574555 | solution.py:30
  78.1 1.3 bitcast_add_fusion.2
  79.4 1.2 bitcast_add_fusion.2
  80.7 1.2 bitcast_add_fusion.2
  82.0 1.0 fusion.62
  83.0 1.5 collective-permute-start.1
  84.7 8.3 %collective-permute-done.1 = bf16[1,4,16,16,128]{4,3,2,1,0:T(8,128)(2,1)S(1)} collective-permute-done((bf16[1,4,16,16,128]{4,3,2,1,0:T(8,128)(2,1)S(1)}, bf16[1,4,16,16,128]{4,3,2,1,0:T(8,128)(2,1)S(1)}, u32[]{:S(2)}, u32[]{:S(2)}) %collective-permute-start.1) | collective-permute-done | bytes 262176 | tf_op jit(solution)/shard_map/ppermute | solution.py:14
  94.9 0.3 fusion.287
  97.2 0.3 fusion.288
  99.4 0.3 fusion.22
  103.3 0.3 fusion.36
  103.8 0.3 fusion.34
  105.8 0.3 fusion.27
  108.3 0.3 fusion.45
  108.9 0.3 fusion.43
  109.2 0.3 fusion.42
  109.4 0.3 fusion.41
  110.0 1.6 pad_maximum_fusion
  111.6 62.5 %all-gather.8.cloned.1.call-done = f32[16,9,128,128]{3,2,1,0:T(8,128)} async-done(((f32[4,9,128,128]{3,2,1,0:T(8,128)}), f32[16,9,128,128]{3,2,1,0:T(8,128)}) %all-gather.8.cloned.1.call-update) | async-done | bytes 9437200 | tf_op jit(solution)/shard_map/all_gather | solution.py:99
  174.1 6.0 %reduce_sum.9 = bf16[4,9,128,128]{3,2,1,0:T(8,128)(2,1)} reduce(f32[4,4,9,128,128]{4,3,2,1,0:T(8,128)} %bitcast.707, f32[]{:T(128)} %constant.62.clone.1), dimensions={0}, to_apply=%region_2.3 | reduce | flops 1769472 | bytes 10616836 | tf_op jit(solution)/shard_map/reduce_sum | solution.py:99
  (108 shorter events, 21.3 us)
Async XLA Ops:
  7.2 13.7 %copy-start.3 = (bf16[1,4,9,128,128]{4,3,2,1,0:T(8,128)(2,1)S(1)}, bf16[1,4,9,128,128]{4,3,2,1,0:T(8,128)(2,1)}, u32[]{:S(2)}) copy-start(bf16[1,4,9,128,128]{4,3,2,1,0:T(8,128)(2,1)} %param.9) | copy-start | bytes 3538948
  7.2 70.8 %all-gather.6.cloned.1.call-start = ((), (), s32[]{:S(2)}) async-start(), calls=%async_computation | async-start | bytes 2621440 | tf_op jit(solution)/shard_map/all_gather | solution.py:21
  7.2 11.6 %collective-permute-start = (bf16[1,4,16,16,128]{4,3,2,1,0:T(8,128)(2,1)}, bf16[1,4,16,16,128]{4,3,2,1,0:T(8,128)(2,1)S(1)}, u32[]{:S(2)}, u32[]{:S(2)}) collective-permute-start(bf16[1,4,16,16,128]{4,3,2,1,0:T(8,128)(2,1)} %param.10), channel_id=1, source_target_pairs={{4,0},{8,4},{12,8},{5,1},{9,5},{13,9},{6,2},{10,6},{14,10},{7,3},{... | collective-permute-start | bytes 786440 | tf_op jit(solution)/shard_map/ppermute | solution.py:14
  22.0 1.2 copy-start
  22.0 1.3 copy-start.2
  29.4 1.0 copy-start.4
  30.4 1.2 copy-start.6
  31.5 142.6 %all-gather.8.cloned.1.call-start = ((), (), s32[]{:S(2)}) async-start(), calls=%async_computation.1 | async-start | bytes 11796480 | tf_op jit(solution)/shard_map/all_gather | solution.py:99
  78.0 3.9 %copy-start.1 = (f32[4,16,16,128]{3,2,1,0:T(8,128)S(1)}, f32[4,16,16,128]{3,2,1,0:T(8,128)}, u32[]{:S(2)}) copy-start(f32[4,16,16,128]{3,2,1,0:T(8,128)} %fusion.12) | copy-start | bytes 1572868
  83.0 10.0 %copy-start.5 = (bf16[1,4,16,16,128]{4,3,2,1,0:T(8,128)(2,1)}, bf16[1,4,16,16,128]{4,3,2,1,0:T(8,128)(2,1)S(1)}, u32[]{:S(2)}) copy-start(bf16[1,4,16,16,128]{4,3,2,1,0:T(8,128)(2,1)S(1)} %fusion.62) | copy-start | bytes 786436
  83.0 9.9 %collective-permute-start.1 = (bf16[1,4,16,16,128]{4,3,2,1,0:T(8,128)(2,1)S(1)}, bf16[1,4,16,16,128]{4,3,2,1,0:T(8,128)(2,1)S(1)}, u32[]{:S(2)}, u32[]{:S(2)}) collective-permute-start(bf16[1,4,16,16,128]{4,3,2,1,0:T(8,128)(2,1)S(1)} %fusion.62), channel_id=1, source_target_pairs={{4,0},{8,4},{12,8},{5,1},{9,5},{13,9},{6,2},{10,6},{14,10},{7,3},{... | collective-permute-start | bytes 786440 | tf_op jit(solution)/shard_map/ppermute | solution.py:14
Sparse Core Ops, SparseCore 0:
  31.6 46.3 all-gather.5
  111.8 62.3 all-gather.7
